TPU v7x, 32 devices: a whole 2x2x4 slice. The times are simulated.
32 devices in a mesh: section: 2 (over x), dp: 4 (over y, core), expert: 4 (over z).
Axes of the slice: x: 2, y: 2, z: 4, core: 2. Of those that a mesh axis runs over, the one named last changes fastest.
Arguments:
- inbound: bfloat16 [2, 16, 256, 1024], P('section', ('dp', 'expert')), may hold values from -6 to 6
- queued: bfloat16 [16, 256, 1024], P(('dp', 'expert')), may hold values from -6 to 6
- routes: int32 [2, 2, 16, 256, 1], P('section', None, ('dp', 'expert')), may hold values from 0 to 3
- first_gain: float32 [2, 1024], P('section'), may hold values from 0.1 to 1.9
- attention_in: bfloat16 [2, 1024, 1536], P('section', 'dp'), may hold values from -3.1875 to 3.1875
- attention_out: bfloat16 [2, 512, 1024], P('section', 'dp'), may hold values from -0.25 to 0.25
- second_gain: float32 [2, 1024], P('section'), may hold values from 0.1 to 1.9
- router: bfloat16 [2, 1024, 4], P('section'), may hold values from -0.375 to 0.375
- expert_in: bfloat16 [2, 4, 1024, 2048], P('section', 'expert', 'dp'), may hold values from -0.1875 to 0.1875
- expert_out: bfloat16 [2, 4, 2048, 1024], P('section', 'expert', 'dp'), may hold values from -0.125 to 0.125
Outputs:
- section_output: bfloat16 [2, 2, 16, 256, 1024], P('section', None, ('dp', 'expert'))
All inputs are finite; a program needn't handle non-finite values.
Results may differ from a plain program's by a relative error of at most 0.0056.
Values may be sent and summed in bfloat16 or wider, within the bound.
A program may use at most 64 MiB of HBM per device.

v0:
```python
from functools import partial
import jax
import jax.numpy as jnp
from jax import lax
from jax.sharding import PartitionSpec as P

HEAD_DIM = 64
CAP = 16
EPSILON = 1e-06


def shifted(shard, axis, by):
    count = lax.axis_size(axis)
    pairs = [(i, i + by) for i in range(count) if 0 <= i + by < count]
    return lax.ppermute(shard, axis, pairs)


def layer_norm(activations, gain_vector):
    widened = activations.astype(jnp.float32)
    centre = widened - jnp.mean(widened, axis=-1, keepdims=True)
    spread = jnp.mean(centre * centre, axis=-1, keepdims=True)
    return (centre * lax.rsqrt(spread + EPSILON) * gain_vector).astype(jnp.bfloat16)


def build_slots(chosen, expert_count):
    onehot = (chosen[:, None] == jnp.arange(expert_count, dtype=jnp.int32)[None, :]).astype(
        jnp.int32
    )
    before = jnp.cumsum(onehot, axis=0) - onehot
    position = jnp.sum(before * onehot, axis=1)
    retained = position < CAP
    slot_index = chosen * CAP + position
    slot_table = (
        slot_index[:, None] == jnp.arange(expert_count * CAP, dtype=jnp.int32)[None, :]
    ) & retained[:, None]
    return (onehot, slot_table, slot_index, retained)


def attend(tokens, gain_vector, project_in, project_out):
    image_count, token_count, model_width = tokens.shape
    head_width = project_out.shape[0]
    head_count = head_width // HEAD_DIM
    normed = layer_norm(tokens, gain_vector)
    mixed_rows = jnp.dot(
        normed.reshape(image_count * token_count, model_width),
        project_in,
        preferred_element_type=jnp.float32,
    ).astype(jnp.bfloat16)
    mixed_rows = mixed_rows.reshape(image_count, token_count, 3, head_count, HEAD_DIM)
    scores = jnp.einsum(
        "ishd,ithd->ihst",
        mixed_rows[:, :, 0],
        mixed_rows[:, :, 1],
        preferred_element_type=jnp.float32,
    ) * HEAD_DIM ** (-0.5)
    softmax_weights = jax.nn.softmax(scores, axis=-1).astype(jnp.bfloat16)
    context = jnp.einsum(
        "ihst,ithd->ishd", softmax_weights, mixed_rows[:, :, 2], preferred_element_type=jnp.float32
    )
    context = context.astype(jnp.bfloat16).reshape(image_count * token_count, head_width)
    branch = jnp.dot(context, project_out, preferred_element_type=jnp.float32).reshape(
        image_count, token_count, model_width
    )
    return (tokens.astype(jnp.float32) + branch).astype(jnp.bfloat16)


def route_and_mix(residual, chosen, gain_vector, router_cols, own_in, own_out):
    image_count, token_count, model_width = residual.shape
    expert_count = router_cols.shape[1]
    normed = layer_norm(residual, gain_vector)
    logits = jnp.dot(
        normed.reshape(image_count * token_count, model_width),
        router_cols,
        preferred_element_type=jnp.float32,
    ).reshape(image_count, token_count, expert_count)
    onehot, slot_table, slot_index, retained = jax.vmap(
        partial(build_slots, expert_count=expert_count)
    )(chosen)
    gating = jax.nn.sigmoid(jnp.sum(logits * onehot.astype(jnp.float32), axis=-1))
    outgoing = jnp.einsum(
        "isk,isd->ikd", slot_table.astype(jnp.bfloat16), normed, preferred_element_type=jnp.float32
    ).astype(jnp.bfloat16)
    outgoing = outgoing.reshape(image_count, expert_count, CAP, model_width)
    arrived = lax.all_to_all(outgoing, "expert", split_axis=1, concat_axis=0, tiled=True)
    flat_rows = arrived.reshape(-1, model_width)
    hidden = jax.nn.gelu(
        jnp.dot(flat_rows, own_in, preferred_element_type=jnp.float32), approximate=False
    ).astype(jnp.bfloat16)
    answer = jnp.dot(hidden, own_out, preferred_element_type=jnp.float32).astype(jnp.bfloat16)
    answered = lax.all_to_all(
        answer.reshape(arrived.shape), "expert", split_axis=0, concat_axis=1, tiled=True
    )
    answered = answered.reshape(image_count, expert_count * CAP, model_width)
    combined = jnp.einsum(
        "isk,ikd->isd",
        slot_table.astype(jnp.bfloat16),
        answered,
        preferred_element_type=jnp.float32,
    )
    return (residual.astype(jnp.float32) + gating[:, :, None] * combined).astype(jnp.bfloat16)


def per_device(
    inbound,
    queued,
    routes,
    first_gain,
    attention_in,
    attention_out,
    second_gain,
    router,
    expert_in,
    expert_out,
):
    section_index = lax.axis_index("section")
    chosen = routes[0, :, :, :, 0]
    full_in, full_out = (
        lax.all_gather(attention_in, "dp", axis=1, tiled=True),
        lax.all_gather(attention_out, "dp", axis=1, tiled=True),
    )
    first_mixed = attend(inbound[0], first_gain[0], full_in[0], full_out[0])
    own_in, own_out = (
        lax.all_gather(expert_in[:, 0], "dp", axis=1, tiled=True),
        lax.all_gather(expert_out[:, 0], "dp", axis=1, tiled=True),
    )
    first_tick = route_and_mix(
        first_mixed, chosen[0], second_gain[0], router[0], own_in[0], own_out[0]
    )
    arrived = shifted(first_tick, "section", 1)
    entering = jnp.where(section_index == 0, queued, arrived)
    second_mixed = attend(entering, first_gain[0], full_in[0], full_out[0])
    second_tick = route_and_mix(
        second_mixed, chosen[1], second_gain[0], router[0], own_in[0], own_out[0]
    )
    return jnp.stack([first_tick, second_tick])[None]


def solution(mesh):
    in_specs = (
        P("section", ("dp", "expert"), None, None),
        P(("dp", "expert"), None, None),
        P("section", None, ("dp", "expert"), None, None),
        P("section", None),
        P("section", "dp", None),
        P("section", "dp", None),
        P("section", None),
        P("section", None, None),
        P("section", "expert", "dp", None),
        P("section", "expert", "dp", None),
    )
    out_specs = P("section", None, ("dp", "expert"), None, None)
    return jax.shard_map(
        per_device, mesh=mesh, in_specs=in_specs, out_specs=out_specs, check_vma=False
    )
```

profile of v0, /device:TPU:0, one launch (start us, length us, event | category | flops | bytes accessed | tf_op | source)
XLA Modules:
  0.0 201.7 jit_solution(5057114900987125693)
XLA Ops:
  6.6 0.7 all-gather.7.cloned.1.call-update
  7.3 0.7 all-gather.9.cloned.1.call-update
  8.1 0.7 all-gather.11.cloned.1.call-update
  8.8 0.5 all-gather.13.cloned.1.call-update
  9.4 1.2 reduce-window.14
  11.1 1.2 reduce-window.16
  12.5 0.1 convert_reduce_fusion
  12.7 0.3 fusion.56
  13.0 27.2 %all-gather.7.cloned.1.call-done = bf16[1,1024,1536]{2,1,0:T(8,128)(2,1)} async-done(((bf16[1,256,1536]{2,1,0:T(8,128)(2,1)}), bf16[1,1024,1536]{2,1,0:T(8,128)(2,1)}) %all-gather.7.cloned.1.call-update) | async-done | bytes 3145744 | tf_op jit(solution)/shard_map/all_gather | solution.py:118
  40.2 3.0 %fusion.14 = bf16[256,1536]{1,0:T(8,128)(2,1)S(1)} fusion(bf16[1,1024,1536]{2,1,0:T(8,128)(2,1)} %all-gather.7.cloned.1.call-done, bf16[1,1,256,1024]{3,2,1,0:T(8,128)(2,1)S(1)} %copy-done.1, f32[1024]{0:T(1024)S(1)} %bitcast.238, f32[256]{0:T(256)S(1)} %add_rsqrt_fusion.3, f32[256]{0:T(256)S(1)} %broadcast_multiply_fusion.3), kind=kOutput, calls=%fused_computation.14 | convolution fusion | flops 807010304 | bytes 4462592 | tf_op jit(solution)/shard_map/dot_general | solution.py:44
  43.2 0.3 copy.33
  43.5 0.8 fusion.262
  44.3 1.1 convolution_convert_fusion.1
  45.4 13.1 %all-gather.9.cloned.1.call-done = bf16[1,512,1024]{2,1,0:T(8,128)(2,1)} async-done(((bf16[1,128,1024]{2,1,0:T(8,128)(2,1)}), bf16[1,512,1024]{2,1,0:T(8,128)(2,1)}) %all-gather.9.cloned.1.call-update) | async-done | bytes 1048592 | tf_op jit(solution)/shard_map/all_gather | solution.py:119
  58.5 1.8 convert_reduce_fusion.3
  60.3 0.3 fusion.48
  60.6 0.3 fusion.50
  60.9 1.0 convolution_convert_fusion.3
  61.9 4.6 %all-to-all-start = ((bf16[1,4,16,1024]{3,2,0,1:T(8,128)(2,1)}), bf16[1,4,16,1024]{3,2,0,1:T(8,128)(2,1)S(1)}, u32[]{:S(2)}, u32[]{:S(2)}) async-start(bf16[1,4,16,1024]{3,2,0,1:T(8,128)(2,1)} %bitcast.22), calls=%async_computation | async-start | bytes 262144 | tf_op jit(solution)/shard_map/all_to_all | solution.py:84
  66.7 0.3 fusion.40
  67.0 5.8 %all-to-all-done = bf16[1,4,16,1024]{3,2,0,1:T(8,128)(2,1)S(1)} async-done(((bf16[1,4,16,1024]{3,2,0,1:T(8,128)(2,1)}), bf16[1,4,16,1024]{3,2,0,1:T(8,128)(2,1)S(1)}, u32[]{:S(2)}, u32[]{:S(2)}) %all-to-all-start) | async-done | bytes 131104 | tf_op jit(solution)/shard_map/all_to_all | solution.py:84
  72.8 21.8 %all-gather.11.cloned.1.call-done = bf16[1,1,1024,2048]{3,2,1,0:T(8,128)(2,1)} async-done(((bf16[1,1,256,2048]{3,2,1,0:T(8,128)(2,1)}), bf16[1,1,1024,2048]{3,2,1,0:T(8,128)(2,1)}) %all-gather.11.cloned.1.call-update) | async-done | bytes 4194320 | tf_op jit(solution)/shard_map/all_gather | solution.py:123
  94.6 35.9 %all-gather.13.cloned.1.call-done = bf16[1,1,2048,1024]{3,2,1,0:T(8,128)(2,1)} async-done(((bf16[1,1,512,1024]{3,2,1,0:T(8,128)(2,1)}), bf16[1,1,2048,1024]{3,2,1,0:T(8,128)(2,1)}) %all-gather.13.cloned.1.call-update) | async-done | bytes 4194320 | tf_op jit(solution)/shard_map/all_gather | solution.py:124
  130.5 6.8 %fusion.34 = bf16[64,1024]{1,0:T(8,128)(2,1)} fusion(bf16[1,1,2048,1024]{3,2,1,0:T(8,128)(2,1)} %all-gather.13.cloned.1.call-done, bf16[64,1024]{1,0:T(8,128)(2,1)S(1)} %bitcast.224, bf16[1,1,1024,2048]{3,2,1,0:T(8,128)(2,1)} %all-gather.11.cloned.1.call-done), kind=kOutput, calls=%fused_computation.55 | convolution fusion | flops 545456128 | bytes 8650752 | tf_op jit(solution)/shard_map/dot_general | solution.py:89
  137.3 4.6 %all-to-all-start.1 = ((bf16[4,1,16,1024]{3,2,1,0:T(8,128)(2,1)}), bf16[4,1,16,1024]{3,2,1,0:T(8,128)(2,1)S(1)}, u32[]{:S(2)}, u32[]{:S(2)}) async-start(bf16[4,1,16,1024]{3,2,1,0:T(8,128)(2,1)} %bitcast.27), calls=%async_computation.1 | async-start | bytes 262144 | tf_op jit(solution)/shard_map/all_to_all | solution.py:90
  142.0 6.3 %all-to-all-done.1 = bf16[4,1,16,1024]{3,2,1,0:T(8,128)(2,1)S(1)} async-done(((bf16[4,1,16,1024]{3,2,1,0:T(8,128)(2,1)}), bf16[4,1,16,1024]{3,2,1,0:T(8,128)(2,1)S(1)}, u32[]{:S(2)}, u32[]{:S(2)}) %all-to-all-start.1) | async-done | bytes 131104 | tf_op jit(solution)/shard_map/all_to_all | solution.py:90
  148.3 0.3 fusion.24
  148.6 3.7 %collective-permute-start = (bf16[1,256,1024]{2,1,0:T(8,128)(2,1)S(1)}, bf16[1,256,1024]{2,1,0:T(8,128)(2,1)S(1)}, u32[]{:S(2)}, u32[]{:S(2)}) collective-permute-start(bf16[1,256,1024]{2,1,0:T(8,128)(2,1)S(1)} %bitcast.216), channel_id=1, source_target_pairs={{0,16},{1,17},{2,18},{3,19},{4,20},{5,21},{6,22},{7,23},{8,24},{9,... | collective-permute-start | bytes 1572872 | tf_op jit(solution)/shard_map/ppermute | solution.py:15
  152.4 9.5 %collective-permute-done = bf16[1,256,1024]{2,1,0:T(8,128)(2,1)S(1)} collective-permute-done((bf16[1,256,1024]{2,1,0:T(8,128)(2,1)S(1)}, bf16[1,256,1024]{2,1,0:T(8,128)(2,1)S(1)}, u32[]{:S(2)}, u32[]{:S(2)}) %collective-permute-start) | collective-permute-done | bytes 524320 | tf_op jit(solution)/shard_map/ppermute | solution.py:15
  161.9 0.2 convert_reduce_fusion.2
  162.2 0.3 fusion.45
  162.5 1.1 fusion.17
  163.6 0.3 copy.39
  163.8 0.8 fusion.263
  164.7 1.1 convolution_convert_fusion
  165.8 0.1 copy-done.6
  165.9 0.5 convert_reduce_fusion.1
  166.4 0.3 fusion.42
  166.7 0.3 fusion.71
  167.1 0.9 convolution_convert_fusion.2
  167.9 3.9 %all-to-all-start.2 = ((bf16[1,4,16,1024]{3,2,0,1:T(8,128)(2,1)}), bf16[1,4,16,1024]{3,2,0,1:T(8,128)(2,1)S(1)}, u32[]{:S(2)}, u32[]{:S(2)}) async-start(bf16[1,4,16,1024]{3,2,0,1:T(8,128)(2,1)} %bitcast.48), calls=%async_computation.2 | async-start | bytes 262144 | tf_op jit(solution)/shard_map/all_to_all | solution.py:84
  171.8 0.3 fusion.41
  172.1 5.7 %all-to-all-done.2 = bf16[1,4,16,1024]{3,2,0,1:T(8,128)(2,1)S(1)} async-done(((bf16[1,4,16,1024]{3,2,0,1:T(8,128)(2,1)}), bf16[1,4,16,1024]{3,2,0,1:T(8,128)(2,1)S(1)}, u32[]{:S(2)}, u32[]{:S(2)}) %all-to-all-start.2) | async-done | bytes 131104 | tf_op jit(solution)/shard_map/all_to_all | solution.py:84
  177.7 6.8 %fusion.37 = bf16[64,1024]{1,0:T(8,128)(2,1)} fusion(bf16[1,1,2048,1024]{3,2,1,0:T(8,128)(2,1)} %all-gather.13.cloned.1.call-done, bf16[64,1024]{1,0:T(8,128)(2,1)S(1)} %bitcast.225, bf16[1,1,1024,2048]{3,2,1,0:T(8,128)(2,1)} %all-gather.11.cloned.1.call-done), kind=kOutput, calls=%fused_computation.56 | convolution fusion | flops 545456128 | bytes 8650752 | tf_op jit(solution)/shard_map/dot_general | solution.py:89
  184.5 3.3 %all-to-all-start.3 = ((bf16[4,1,16,1024]{3,2,1,0:T(8,128)(2,1)}), bf16[4,1,16,1024]{3,2,1,0:T(8,128)(2,1)S(1)}, u32[]{:S(2)}, u32[]{:S(2)}) async-start(bf16[4,1,16,1024]{3,2,1,0:T(8,128)(2,1)} %bitcast.51), calls=%async_computation.3 | async-start | bytes 262144 | tf_op jit(solution)/shard_map/all_to_all | solution.py:90
  187.8 5.9 %all-to-all-done.3 = bf16[4,1,16,1024]{3,2,1,0:T(8,128)(2,1)S(1)} async-done(((bf16[4,1,16,1024]{3,2,1,0:T(8,128)(2,1)}), bf16[4,1,16,1024]{3,2,1,0:T(8,128)(2,1)S(1)}, u32[]{:S(2)}, u32[]{:S(2)}) %all-to-all-start.3) | async-done | bytes 131104 | tf_op jit(solution)/shard_map/all_to_all | solution.py:90
  193.7 0.3 fusion.33
  194.1 1.1 maximum_bitcast_fusion
  (56 shorter events, 1.2 us)
Async XLA Ops:
  6.5 60.2 %copy-start = (bf16[1,1024,4]{1,2,0:T(4,128)(2,1)S(1)}, bf16[1,1024,4]{1,2,0:T(4,128)(2,1)}, u32[]{:S(2)}) copy-start(bf16[1,1024,4]{1,2,0:T(4,128)(2,1)} %param.17) | copy-start | bytes 24580
  6.5 2.8 %copy-start.4 = (s32[1,2,1,256,1]{3,4,2,1,0:T(1,128)S(1)}, s32[1,2,1,256,1]{3,4,2,1,0:T(1,128)}, u32[]{:S(2)}) copy-start(s32[1,2,1,256,1]{3,4,2,1,0:T(1,128)} %param.12) | copy-start | bytes 6148
  6.5 6.0 %copy-start.1 = (bf16[1,1,256,1024]{3,2,1,0:T(8,128)(2,1)S(1)}, bf16[1,1,256,1024]{3,2,1,0:T(8,128)(2,1)}, u32[]{:S(2)}) copy-start(bf16[1,1,256,1024]{3,2,1,0:T(8,128)(2,1)} %param.10) | copy-start | bytes 1572868
  6.5 33.7 %copy-start.7 = (f32[1,1024]{1,0:T(1,128)S(1)}, f32[1,1024]{1,0:T(1,128)}, u32[]{:S(2)}) copy-start(f32[1,1024]{1,0:T(1,128)} %param.13) | copy-start | bytes 12292
  6.5 33.7 %all-gather.7.cloned.1.call-start = ((), (), s32[]{:S(2)}) async-start(), calls=%async_computation.4 | async-start | bytes 3932160 | tf_op jit(solution)/shard_map/all_gather | solution.py:118
  7.3 51.2 %all-gather.9.cloned.1.call-start = ((), (), s32[]{:S(2)}) async-start(), calls=%async_computation.5 | async-start | bytes 1310720 | tf_op jit(solution)/shard_map/all_gather | solution.py:119
  8.0 86.6 %all-gather.11.cloned.1.call-start = ((), (), s32[]{:S(2)}) async-start(), calls=%async_computation.6 | async-start | bytes 5242880 | tf_op jit(solution)/shard_map/all_gather | solution.py:123
  8.8 121.8 %all-gather.13.cloned.1.call-start = ((), (), s32[]{:S(2)}) async-start(), calls=%async_computation.7 | async-start | bytes 5242880 | tf_op jit(solution)/shard_map/all_gather | solution.py:124
  45.4 15.2 %copy-start.3 = (f32[1,1024]{1,0:T(1,128)S(1)}, f32[1,1024]{1,0:T(1,128)}, u32[]{:S(2)}) copy-start(f32[1,1024]{1,0:T(1,128)} %param.16) | copy-start | bytes 12292
  61.9 10.9 %all-to-all-start = ((bf16[1,4,16,1024]{3,2,0,1:T(8,128)(2,1)}), bf16[1,4,16,1024]{3,2,0,1:T(8,128)(2,1)S(1)}, u32[]{:S(2)}, u32[]{:S(2)}) async-start(bf16[1,4,16,1024]{3,2,0,1:T(8,128)(2,1)} %bitcast.22), calls=%async_computation | async-start | bytes 262144 | tf_op jit(solution)/shard_map/all_to_all | solution.py:84
  130.5 31.4 %copy-start.2 = (bf16[1,256,1024]{2,1,0:T(8,128)(2,1)S(1)}, bf16[1,256,1024]{2,1,0:T(8,128)(2,1)}, u32[]{:S(2)}) copy-start(bf16[1,256,1024]{2,1,0:T(8,128)(2,1)} %param.11) | copy-start | bytes 1572868
  137.3 10.9 %all-to-all-start.1 = ((bf16[4,1,16,1024]{3,2,1,0:T(8,128)(2,1)}), bf16[4,1,16,1024]{3,2,1,0:T(8,128)(2,1)S(1)}, u32[]{:S(2)}, u32[]{:S(2)}) async-start(bf16[4,1,16,1024]{3,2,1,0:T(8,128)(2,1)} %bitcast.27), calls=%async_computation.1 | async-start | bytes 262144 | tf_op jit(solution)/shard_map/all_to_all | solution.py:90
  148.3 14.2 %copy-start.5 = (bf16[1,1024,1536]{2,1,0:T(8,128)(2,1)S(1)}, bf16[1,1024,1536]{2,1,0:T(8,128)(2,1)}, u32[]{:S(2)}) copy-start(bf16[1,1024,1536]{2,1,0:T(8,128)(2,1)} %all-gather.7.cloned.1.call-done) | copy-start | bytes 9437188
  148.6 13.3 %collective-permute-start = (bf16[1,256,1024]{2,1,0:T(8,128)(2,1)S(1)}, bf16[1,256,1024]{2,1,0:T(8,128)(2,1)S(1)}, u32[]{:S(2)}, u32[]{:S(2)}) collective-permute-start(bf16[1,256,1024]{2,1,0:T(8,128)(2,1)S(1)} %bitcast.216), channel_id=1, source_target_pairs={{0,16},{1,17},{2,18},{3,19},{4,20},{5,21},{6,22},{7,23},{8,24},{9,... | collective-permute-start | bytes 1572872 | tf_op jit(solution)/shard_map/ppermute | solution.py:15
  164.7 1.2 copy-start.6
  167.9 9.8 %all-to-all-start.2 = ((bf16[1,4,16,1024]{3,2,0,1:T(8,128)(2,1)}), bf16[1,4,16,1024]{3,2,0,1:T(8,128)(2,1)S(1)}, u32[]{:S(2)}, u32[]{:S(2)}) async-start(bf16[1,4,16,1024]{3,2,0,1:T(8,128)(2,1)} %bitcast.48), calls=%async_computation.2 | async-start | bytes 262144 | tf_op jit(solution)/shard_map/all_to_all | solution.py:84
  184.5 9.2 %all-to-all-start.3 = ((bf16[4,1,16,1024]{3,2,1,0:T(8,128)(2,1)}), bf16[4,1,16,1024]{3,2,1,0:T(8,128)(2,1)S(1)}, u32[]{:S(2)}, u32[]{:S(2)}) async-start(bf16[4,1,16,1024]{3,2,1,0:T(8,128)(2,1)} %bitcast.51), calls=%async_computation.3 | async-start | bytes 262144 | tf_op jit(solution)/shard_map/all_to_all | solution.py:90
Sparse Core Ops, SparseCore 0:
  8.9 31.2 all-gather.6
  41.8 16.7 all-gather.8
  60.1 34.4 all-gather.10
  96.0 34.4 all-gather.12
where the time goes:
time: 202 us
  waiting for transfers between devices  134 us (66%)
  matrix products  26.9 us (13%)
  starting transfers between devices  20.3 us (10%)
  between operations  13.3 us (7%)
  other arithmetic  5.87 us (3%)
    all_gather x1, waiting for transfers between devices, per_device(): lax.all_gather(expert_out[:, 0], 'dp', axis=1, tiled=True)  35.9 us
    all_gather x1, waiting for transfers between devices, per_device(): lax.all_gather(attention_in, 'dp', axis=1, tiled=True)  27.2 us
    all_gather x1, waiting for transfers between devices, per_device(): lax.all_gather(expert_in[:, 0], 'dp', axis=1, tiled=True)  21.8 us
    dot_general x2, matrix products, route_and_mix(): jnp.dot(hidden, own_out, preferred_element_type=jnp.float32)  13.6 us
    all_gather x1, waiting for transfers between devices, per_device(): lax.all_gather(attention_out, 'dp', axis=1, tiled=True)  13.1 us
    all_to_all x2, waiting for transfers between devices, route_and_mix(): lax.all_to_all(answer.reshape(arrived.shape), 'expert', split_axis=0, con...  12.2 us
    all_to_all x2, waiting for transfers between devices, route_and_mix(): lax.all_to_all(outgoing, 'expert', split_axis=1, concat_axis=0, tiled=True)  11.5 us
    ppermute x1, waiting for transfers between devices, shifted(): return lax.ppermute(shard, axis, pairs)  9.51 us
  transfers between devices with their start and end apart: 9, of which 9 were waited for; matrix products, arithmetic and copies ran while one was open for 6% of the time, Pallas kernels for 0%

commit v1 on v0

--- a/solution.py
+++ b/solution.py
@@ -119,9 +119,26 @@
         lax.all_gather(attention_out, "dp", axis=1, tiled=True),
     )
     first_mixed = attend(inbound[0], first_gain[0], full_in[0], full_out[0])
+
+    def order_blocks(panel):
+        long_array = jax.lax.axis_size("dp")
+        big, r_now = (long_array, jax.lax.axis_index("dp"))
+        piece_next, last = (panel, 1)
+        while last < big:
+            z2 = jax.lax.ppermute(
+                piece_next,
+                axis_name="dp",
+                perm=tuple(((src_i, src_i ^ last) for src_i in range(big))),
+            )
+            arr_now = jnp.concatenate([piece_next, z2], axis=1)
+            r2 = jnp.concatenate([z2, piece_next], axis=1)
+            piece_next = jnp.where(r_now & last == 0, arr_now, r2)
+            last = 2 * last
+        return piece_next
+
     own_in, own_out = (
         lax.all_gather(expert_in[:, 0], "dp", axis=1, tiled=True),
-        lax.all_gather(expert_out[:, 0], "dp", axis=1, tiled=True),
+        order_blocks(expert_out[:, 0]),
     )
     first_tick = route_and_mix(
         first_mixed, chosen[0], second_gain[0], router[0], own_in[0], own_out[0]

time: 202 us -> 192 us (0.950)
  waiting for transfers between devices: 134 us -> 110 us
  matrix products: 26.9 us -> 32.1 us
  other arithmetic: 5.87 us -> 10.6 us
  starting transfers between devices: 20.3 us -> 23.3 us
    all_gather x1 -> x0, waiting for transfers between devices: 35.9 us -> none  [per_device(): lax.all_gather(expert_out[:, 0], 'dp', axis=1, tiled=True)]
    all_gather x1, waiting for transfers between devices: 27.2 us -> 39 us  [per_device(): lax.all_gather(attention_in, 'dp', axis=1, tiled=True)]
    select_n x0 -> x2, other arithmetic: none -> 4.76 us  [order_blocks(): piece_next = jnp.where(r_now & last == 0, arr_now, r2)]
    ppermute x0 -> x2, starting transfers between devices: none -> 3.07 us  [order_blocks(): jax.lax.ppermute(piece_next, axis_name='dp', perm=tuple(((src_i, src_i ^...]
    all_gather x1, waiting for transfers between devices: 13.1 us -> 16.1 us  [per_device(): lax.all_gather(attention_out, 'dp', axis=1, tiled=True)]
    dot_general x2, matrix products: 13.6 us -> 15.7 us  [route_and_mix(): jnp.dot(hidden, own_out, preferred_element_type=jnp.float32)]
    all_to_all x2, waiting for transfers between devices: 11.5 us -> 9.36 us  [route_and_mix(): lax.all_to_all(outgoing, 'expert', split_axis=1, concat_axis=0, tiled=True)]
  transfers between devices with their start and end apart: 9 -> 10, of which waited for: 9 -> 8; matrix products, arithmetic and copies ran while one was open for 6% -> 11% of each run, Pallas kernels for 0% -> 0%
where the time goes in v1:
time: 192 us
  waiting for transfers between devices  110 us (57%)
  matrix products  32.1 us (17%)
  starting transfers between devices  23.3 us (12%)
  between operations  13.4 us (7%)
  other arithmetic  10.6 us (6%)
  local copies, waits for them, and re-layouts  2.27 us (1%)
    all_gather x1, waiting for transfers between devices, per_device(): lax.all_gather(attention_in, 'dp', axis=1, tiled=True)  39 us
    all_gather x1, waiting for transfers between devices, per_device(): lax.all_gather(expert_in[:, 0], 'dp', axis=1, tiled=True)  21.7 us
    all_gather x1, waiting for transfers between devices, per_device(): lax.all_gather(attention_out, 'dp', axis=1, tiled=True)  16.1 us
    dot_general x2, matrix products, route_and_mix(): jnp.dot(hidden, own_out, preferred_element_type=jnp.float32)  15.7 us
    all_to_all x2, waiting for transfers between devices, route_and_mix(): lax.all_to_all(answer.reshape(arrived.shape), 'expert', split_axis=0, con...  12.2 us
    ppermute x1, waiting for transfers between devices, shifted(): return lax.ppermute(shard, axis, pairs)  9.51 us
    all_to_all x2, waiting for transfers between devices, route_and_mix(): lax.all_to_all(outgoing, 'expert', split_axis=1, concat_axis=0, tiled=True)  9.36 us
    all_to_all x2, starting transfers between devices, route_and_mix(): lax.all_to_all(outgoing, 'expert', split_axis=1, concat_axis=0, tiled=True)  8.49 us
  transfers between devices with their start and end apart: 10, of which 8 were waited for; matrix products, arithmetic and copies ran while one was open for 11% of the time, Pallas kernels for 0%

profile of v1, /device:TPU:0, one launch (start us, length us, event | category | flops | bytes accessed | tf_op | source)
XLA Modules:
  0.0 191.6 jit_solution(7888486895253215492)
XLA Ops:
  6.6 0.7 all-gather.5.cloned.1.call-update
  7.3 0.7 all-gather.7.cloned.1.call-update
  8.1 0.7 all-gather.9.cloned.1.call-update
  8.8 0.5 collective-permute-start
  9.3 1.2 reduce-window.14
  11.0 1.2 reduce-window.16
  12.8 0.3 fusion.46
  13.2 2.4 %maximum_select_fusion.2 = bf16[1,1024,1024]{2,1,0:T(8,128)(2,1)} fusion(bf16[1,512,1024]{2,1,0:T(8,128)(2,1)S(1)} %collective-permute-done, bf16[1,512,1024]{2,1,0:T(8,128)(2,1)S(1)} %bitcast.212, pred[]{:T(512)S(6)} %eq.160), kind=kLoop, calls=%fused_computation.14 | loop fusion | flops 9437184 | bytes 4194305 | tf_op jit(solution)/shard_map/jit(_where)/select_n | solution.py:135
  15.6 2.5 %collective-permute-start.1 = (bf16[1,1024,1024]{2,1,0:T(8,128)(2,1)}, bf16[1,1024,1024]{2,1,0:T(8,128)(2,1)}, u32[]{:S(2)}, u32[]{:S(2)}) collective-permute-start(bf16[1,1024,1024]{2,1,0:T(8,128)(2,1)} %maximum_select_fusion.2), channel_id=1, source_target_pairs={{0,8},{4,12},{8,0},{12,4},{1,9},{5,13},{9,1},{13,5},{2,10},{6,14},... | collective-permute-start | bytes 6291464 | tf_op jit(solution)/shard_map/ppermute | solution.py:128
  18.1 39.0 %all-gather.5.cloned.1.call-done = bf16[1,1024,1536]{2,1,0:T(8,128)(2,1)} async-done(((bf16[1,256,1536]{2,1,0:T(8,128)(2,1)}), bf16[1,1024,1536]{2,1,0:T(8,128)(2,1)}) %all-gather.5.cloned.1.call-update) | async-done | bytes 3145744 | tf_op jit(solution)/shard_map/all_gather | solution.py:118
  57.2 3.0 %fusion.10 = bf16[256,1536]{1,0:T(8,128)(2,1)S(1)} fusion(bf16[1,1024,1536]{2,1,0:T(8,128)(2,1)} %all-gather.5.cloned.1.call-done, bf16[1,1,256,1024]{3,2,1,0:T(8,128)(2,1)S(1)} %copy-done.3, f32[1024]{0:T(1024)S(1)} %bitcast.237, f32[256]{0:T(256)S(1)} %add_rsqrt_fusion.3, f32[256]{0:T(256)S(1)} %broadcast_multiply_fusion.3), kind=kOutput, calls=%fused_computation.11 | convolution fusion | flops 807010304 | bytes 4462592 | tf_op jit(solution)/shard_map/dot_general | solution.py:44
  60.2 1.2 copy.33
  61.3 1.9 %fusion.254 = f32[8,256]{1,0:T(8,128)S(1)} fusion(bf16[1,256,3,8,64]{1,4,3,2,0:T(8,128)(2,1)} %bitcast.217), kind=kOutput, calls=%fused_computation.313 | convolution fusion | flops 68681984 | bytes 532480 | tf_op jit(solution)/shard_map/sub | solution.py:56
  63.2 1.8 convolution_convert_fusion.1
  65.0 16.1 %all-gather.7.cloned.1.call-done = bf16[1,512,1024]{2,1,0:T(8,128)(2,1)} async-done(((bf16[1,128,1024]{2,1,0:T(8,128)(2,1)}), bf16[1,512,1024]{2,1,0:T(8,128)(2,1)}) %all-gather.7.cloned.1.call-update) | async-done | bytes 1048592 | tf_op jit(solution)/shard_map/all_gather | solution.py:119
  81.1 1.9 convert_reduce_fusion.3
  83.0 0.3 fusion.38
  83.3 0.3 fusion.40
  83.6 1.0 convolution_convert_fusion.5
  84.6 4.6 %all-to-all-start = ((bf16[1,4,16,1024]{3,2,0,1:T(8,128)(2,1)}), bf16[1,4,16,1024]{3,2,0,1:T(8,128)(2,1)S(1)}, u32[]{:S(2)}, u32[]{:S(2)}) async-start(bf16[1,4,16,1024]{3,2,0,1:T(8,128)(2,1)} %bitcast.22), calls=%async_computation | async-start | bytes 262144 | tf_op jit(solution)/shard_map/all_to_all | solution.py:84
  89.2 2.3 %maximum_select_fusion.1 = bf16[1024,1024]{1,0:T(8,128)(2,1)} fusion(bf16[512,1024]{1,0:T(8,128)(2,1)S(1)} %bitcast.214, bf16[512,1024]{1,0:T(8,128)(2,1)S(1)} %bitcast.213, pred[]{:T(512)S(6)} %eq.160), kind=kLoop, calls=%fused_computation.13 | loop fusion | flops 9437184 | bytes 4194305 | tf_op jit(solution)/shard_map/jit(_where)/select_n | solution.py:135
  91.5 0.3 fusion.30
  91.8 3.7 %all-to-all-done = bf16[1,4,16,1024]{3,2,0,1:T(8,128)(2,1)S(1)} async-done(((bf16[1,4,16,1024]{3,2,0,1:T(8,128)(2,1)}), bf16[1,4,16,1024]{3,2,0,1:T(8,128)(2,1)S(1)}, u32[]{:S(2)}, u32[]{:S(2)}) %all-to-all-start) | async-done | bytes 131104 | tf_op jit(solution)/shard_map/all_to_all | solution.py:84
  95.5 21.7 %all-gather.9.cloned.1.call-done = bf16[1,1,1024,2048]{3,2,1,0:T(8,128)(2,1)} async-done(((bf16[1,1,256,2048]{3,2,1,0:T(8,128)(2,1)}), bf16[1,1,1024,2048]{3,2,1,0:T(8,128)(2,1)}) %all-gather.9.cloned.1.call-update) | async-done | bytes 4194320 | tf_op jit(solution)/shard_map/all_gather | solution.py:140
  117.2 8.5 %convolution_convert_fusion.4 = bf16[64,1024]{1,0:T(8,128)(2,1)} fusion(bf16[1024,1024]{1,0:T(8,128)(2,1)} %bitcast.28, bf16[1024,1024]{1,0:T(8,128)(2,1)} %maximum_select_fusion.1, pred[]{:T(512)S(6)} %eq.159, bf16[64,1024]{1,0:T(8,128)(2,1)S(1)} %bitcast.223, bf16[1,1,1024,2048]{3,2,1,0:T(8,128)(2,1)} %all-gather.9.cloned.1.call-done), kind=kOutput, calls=%fused_computation.56 | convolution fusion | flops 564330496 | bytes 8650753 | tf_op jit(solution)/shard_map/dot_general | solution.py:89
  125.7 4.6 %all-to-all-start.1 = ((bf16[4,1,16,1024]{3,2,1,0:T(8,128)(2,1)}), bf16[4,1,16,1024]{3,2,1,0:T(8,128)(2,1)S(1)}, u32[]{:S(2)}, u32[]{:S(2)}) async-start(bf16[4,1,16,1024]{3,2,1,0:T(8,128)(2,1)} %bitcast.30), calls=%async_computation.1 | async-start | bytes 262144 | tf_op jit(solution)/shard_map/all_to_all | solution.py:90
  130.3 6.3 %all-to-all-done.1 = bf16[4,1,16,1024]{3,2,1,0:T(8,128)(2,1)S(1)} async-done(((bf16[4,1,16,1024]{3,2,1,0:T(8,128)(2,1)}), bf16[4,1,16,1024]{3,2,1,0:T(8,128)(2,1)S(1)}, u32[]{:S(2)}, u32[]{:S(2)}) %all-to-all-start.1) | async-done | bytes 131104 | tf_op jit(solution)/shard_map/all_to_all | solution.py:90
  136.6 0.3 fusion.20
  137.0 3.7 %collective-permute-start.2 = (bf16[1,256,1024]{2,1,0:T(8,128)(2,1)S(1)}, bf16[1,256,1024]{2,1,0:T(8,128)(2,1)S(1)}, u32[]{:S(2)}, u32[]{:S(2)}) collective-permute-start(bf16[1,256,1024]{2,1,0:T(8,128)(2,1)S(1)} %bitcast.215), channel_id=1, source_target_pairs={{0,16},{1,17},{2,18},{3,19},{4,20},{5,21},{6,22},{7,23},{8,24},{9,... | collective-permute-start | bytes 1572872 | tf_op jit(solution)/shard_map/ppermute | solution.py:15
  140.7 9.5 %collective-permute-done.2 = bf16[1,256,1024]{2,1,0:T(8,128)(2,1)S(1)} collective-permute-done((bf16[1,256,1024]{2,1,0:T(8,128)(2,1)S(1)}, bf16[1,256,1024]{2,1,0:T(8,128)(2,1)S(1)}, u32[]{:S(2)}, u32[]{:S(2)}) %collective-permute-start.2) | collective-permute-done | bytes 524320 | tf_op jit(solution)/shard_map/ppermute | solution.py:15
  150.3 0.2 convert_reduce_fusion.2
  150.5 0.3 fusion.35
  150.8 1.1 fusion.13
  151.9 0.3 copy.39
  152.2 0.8 fusion.255
  153.0 1.1 convolution_convert_fusion
  154.1 1.8 convert_reduce_fusion.1
  155.9 0.3 fusion.32
  156.2 0.3 fusion.61
  156.5 0.9 convolution_convert_fusion.3
  157.4 3.9 %all-to-all-start.2 = ((bf16[1,4,16,1024]{3,2,0,1:T(8,128)(2,1)}), bf16[1,4,16,1024]{3,2,0,1:T(8,128)(2,1)S(1)}, u32[]{:S(2)}, u32[]{:S(2)}) async-start(bf16[1,4,16,1024]{3,2,0,1:T(8,128)(2,1)} %bitcast.51), calls=%async_computation.2 | async-start | bytes 262144 | tf_op jit(solution)/shard_map/all_to_all | solution.py:84
  161.3 0.3 fusion.31
  161.5 5.7 %all-to-all-done.2 = bf16[1,4,16,1024]{3,2,0,1:T(8,128)(2,1)S(1)} async-done(((bf16[1,4,16,1024]{3,2,0,1:T(8,128)(2,1)}), bf16[1,4,16,1024]{3,2,0,1:T(8,128)(2,1)S(1)}, u32[]{:S(2)}, u32[]{:S(2)}) %all-to-all-start.2) | async-done | bytes 131104 | tf_op jit(solution)/shard_map/all_to_all | solution.py:84
  167.2 7.3 %convolution_convert_fusion.2 = bf16[64,1024]{1,0:T(8,128)(2,1)} fusion(bf16[1024,1024]{1,0:T(8,128)(2,1)} %bitcast.28, bf16[1024,1024]{1,0:T(8,128)(2,1)S(1)} %copy-done.2, pred[]{:T(512)S(6)} %eq.159, bf16[64,1024]{1,0:T(8,128)(2,1)S(1)} %bitcast.224, bf16[1,1,1024,2048]{3,2,1,0:T(8,128)(2,1)} %all-gather.9.cloned.1.call-done), kind=kOutput, calls=%fused_computation.54 | convolution fusion | flops 564330496 | bytes 8650753 | tf_op jit(solution)/shard_map/dot_general | solution.py:89
  174.5 3.3 %all-to-all-start.3 = ((bf16[4,1,16,1024]{3,2,1,0:T(8,128)(2,1)}), bf16[4,1,16,1024]{3,2,1,0:T(8,128)(2,1)S(1)}, u32[]{:S(2)}, u32[]{:S(2)}) async-start(bf16[4,1,16,1024]{3,2,1,0:T(8,128)(2,1)} %bitcast.54), calls=%async_computation.3 | async-start | bytes 262144 | tf_op jit(solution)/shard_map/all_to_all | solution.py:90
  177.8 5.9 %all-to-all-done.3 = bf16[4,1,16,1024]{3,2,1,0:T(8,128)(2,1)S(1)} async-done(((bf16[4,1,16,1024]{3,2,1,0:T(8,128)(2,1)}), bf16[4,1,16,1024]{3,2,1,0:T(8,128)(2,1)S(1)}, u32[]{:S(2)}, u32[]{:S(2)}) %all-to-all-start.3) | async-done | bytes 131104 | tf_op jit(solution)/shard_map/all_to_all | solution.py:90
  183.7 0.3 fusion.29
  184.0 1.1 maximum_bitcast_fusion
  (67 shorter events, 1.3 us)
Async XLA Ops:
  6.5 85.0 %copy-start = (bf16[1,1024,4]{1,2,0:T(4,128)(2,1)S(1)}, bf16[1,1024,4]{1,2,0:T(4,128)(2,1)}, u32[]{:S(2)}) copy-start(bf16[1,1024,4]{1,2,0:T(4,128)(2,1)} %param.17) | copy-start | bytes 24580
  6.5 2.2 %copy-start.1 = (bf16[1,1,512,1024]{3,2,1,0:T(8,128)(2,1)S(1)}, bf16[1,1,512,1024]{3,2,1,0:T(8,128)(2,1)}, u32[]{:S(2)}) copy-start(bf16[1,1,512,1024]{3,2,1,0:T(8,128)(2,1)} %param.19) | copy-start | bytes 3145732
  6.5 2.7 %copy-start.9 = (s32[1,2,1,256,1]{3,4,2,1,0:T(1,128)S(1)}, s32[1,2,1,256,1]{3,4,2,1,0:T(1,128)}, u32[]{:S(2)}) copy-start(s32[1,2,1,256,1]{3,4,2,1,0:T(1,128)} %param.12) | copy-start | bytes 6148
  6.5 5.9 %copy-start.3 = (bf16[1,1,256,1024]{3,2,1,0:T(8,128)(2,1)S(1)}, bf16[1,1,256,1024]{3,2,1,0:T(8,128)(2,1)}, u32[]{:S(2)}) copy-start(bf16[1,1,256,1024]{3,2,1,0:T(8,128)(2,1)} %param.10) | copy-start | bytes 1572868
  6.5 50.6 %all-gather.5.cloned.1.call-start = ((), (), s32[]{:S(2)}) async-start(), calls=%async_computation.4 | async-start | bytes 3932160 | tf_op jit(solution)/shard_map/all_gather | solution.py:118
  7.3 73.9 %all-gather.7.cloned.1.call-start = ((), (), s32[]{:S(2)}) async-start(), calls=%async_computation.5 | async-start | bytes 1310720 | tf_op jit(solution)/shard_map/all_gather | solution.py:119
  8.0 109.2 %all-gather.9.cloned.1.call-start = ((), (), s32[]{:S(2)}) async-start(), calls=%async_computation.6 | async-start | bytes 5242880 | tf_op jit(solution)/shard_map/all_gather | solution.py:140
  8.8 4.4 %collective-permute-start = (bf16[1,512,1024]{2,1,0:T(8,128)(2,1)S(1)}, bf16[1,512,1024]{2,1,0:T(8,128)(2,1)S(1)}, u32[]{:S(2)}, u32[]{:S(2)}) collective-permute-start(bf16[1,512,1024]{2,1,0:T(8,128)(2,1)S(1)} %bitcast.211), channel_id=1, source_target_pairs={{0,4},{4,0},{8,12},{12,8},{1,5},{5,1},{9,13},{13,9},{2,6},{6,2},{1... | collective-permute-start | bytes 3145736 | tf_op jit(solution)/shard_map/ppermute | solution.py:128
  13.1 44.0 %copy-start.11 = (f32[1,1024]{1,0:T(1,128)S(1)}, f32[1,1024]{1,0:T(1,128)}, u32[]{:S(2)}) copy-start(f32[1,1024]{1,0:T(1,128)} %param.13) | copy-start | bytes 12292
  15.6 76.2 %collective-permute-start.1 = (bf16[1,1024,1024]{2,1,0:T(8,128)(2,1)}, bf16[1,1024,1024]{2,1,0:T(8,128)(2,1)}, u32[]{:S(2)}, u32[]{:S(2)}) collective-permute-start(bf16[1,1024,1024]{2,1,0:T(8,128)(2,1)} %maximum_select_fusion.2), channel_id=1, source_target_pairs={{0,8},{4,12},{8,0},{12,4},{1,9},{5,13},{9,1},{13,5},{2,10},{6,14},... | collective-permute-start | bytes 6291464 | tf_op jit(solution)/shard_map/ppermute | solution.py:128
  61.3 1.9 %copy-start.6 = (bf16[256,1536]{0,1:T(8,128)(2,1)S(1)}, bf16[256,1536]{0,1:T(8,128)(2,1)}, u32[]{:S(2)}) copy-start(bf16[256,1536]{0,1:T(8,128)(2,1)} %copy.33) | copy-start | bytes 2359300
  65.0 18.3 %copy-start.8 = (f32[1,1024]{1,0:T(1,128)S(1)}, f32[1,1024]{1,0:T(1,128)}, u32[]{:S(2)}) copy-start(f32[1,1024]{1,0:T(1,128)} %param.16) | copy-start | bytes 12292
  84.6 10.9 %all-to-all-start = ((bf16[1,4,16,1024]{3,2,0,1:T(8,128)(2,1)}), bf16[1,4,16,1024]{3,2,0,1:T(8,128)(2,1)S(1)}, u32[]{:S(2)}, u32[]{:S(2)}) async-start(bf16[1,4,16,1024]{3,2,0,1:T(8,128)(2,1)} %bitcast.22), calls=%async_computation | async-start | bytes 262144 | tf_op jit(solution)/shard_map/all_to_all | solution.py:84
  117.2 33.0 %copy-start.7 = (bf16[1,256,1024]{2,1,0:T(8,128)(2,1)S(1)}, bf16[1,256,1024]{2,1,0:T(8,128)(2,1)}, u32[]{:S(2)}) copy-start(bf16[1,256,1024]{2,1,0:T(8,128)(2,1)} %param.11) | copy-start | bytes 1572868
  125.7 10.9 %all-to-all-start.1 = ((bf16[4,1,16,1024]{3,2,1,0:T(8,128)(2,1)}), bf16[4,1,16,1024]{3,2,1,0:T(8,128)(2,1)S(1)}, u32[]{:S(2)}, u32[]{:S(2)}) async-start(bf16[4,1,16,1024]{3,2,1,0:T(8,128)(2,1)} %bitcast.30), calls=%async_computation.1 | async-start | bytes 262144 | tf_op jit(solution)/shard_map/all_to_all | solution.py:90
  136.6 14.2 %copy-start.10 = (bf16[1,1024,1536]{2,1,0:T(8,128)(2,1)S(1)}, bf16[1,1024,1536]{2,1,0:T(8,128)(2,1)}, u32[]{:S(2)}) copy-start(bf16[1,1024,1536]{2,1,0:T(8,128)(2,1)} %all-gather.5.cloned.1.call-done) | copy-start | bytes 9437188
  137.0 15.0 %copy-start.4 = (bf16[256,1024]{1,0:T(8,128)(2,1)}, bf16[256,1024]{1,0:T(8,128)(2,1)S(1)}, u32[]{:S(2)}) copy-start(bf16[256,1024]{1,0:T(8,128)(2,1)S(1)} %fusion.20) | copy-start | bytes 1572868
  137.0 13.3 %collective-permute-start.2 = (bf16[1,256,1024]{2,1,0:T(8,128)(2,1)S(1)}, bf16[1,256,1024]{2,1,0:T(8,128)(2,1)S(1)}, u32[]{:S(2)}, u32[]{:S(2)}) collective-permute-start(bf16[1,256,1024]{2,1,0:T(8,128)(2,1)S(1)} %bitcast.215), channel_id=1, source_target_pairs={{0,16},{1,17},{2,18},{3,19},{4,20},{5,21},{6,22},{7,23},{8,24},{9,... | collective-permute-start | bytes 1572872 | tf_op jit(solution)/shard_map/ppermute | solution.py:15
  155.9 11.3 %copy-start.2 = (bf16[1024,1024]{1,0:T(8,128)(2,1)S(1)}, bf16[1024,1024]{1,0:T(8,128)(2,1)}, u32[]{:S(2)}) copy-start(bf16[1024,1024]{1,0:T(8,128)(2,1)} %maximum_select_fusion.1) | copy-start | bytes 6291460
  157.4 9.8 %all-to-all-start.2 = ((bf16[1,4,16,1024]{3,2,0,1:T(8,128)(2,1)}), bf16[1,4,16,1024]{3,2,0,1:T(8,128)(2,1)S(1)}, u32[]{:S(2)}, u32[]{:S(2)}) async-start(bf16[1,4,16,1024]{3,2,0,1:T(8,128)(2,1)} %bitcast.51), calls=%async_computation.2 | async-start | bytes 262144 | tf_op jit(solution)/shard_map/all_to_all | solution.py:84
  167.2 16.8 %copy-start.5 = (bf16[256,1024]{1,0:T(8,128)(2,1)S(1)}, bf16[256,1024]{1,0:T(8,128)(2,1)}, u32[]{:S(2)}) copy-start(bf16[256,1024]{1,0:T(8,128)(2,1)} %copy-done.4) | copy-start | bytes 1572868
  174.5 9.2 %all-to-all-start.3 = ((bf16[4,1,16,1024]{3,2,1,0:T(8,128)(2,1)}), bf16[4,1,16,1024]{3,2,1,0:T(8,128)(2,1)S(1)}, u32[]{:S(2)}, u32[]{:S(2)}) async-start(bf16[4,1,16,1024]{3,2,1,0:T(8,128)(2,1)} %bitcast.54), calls=%async_computation.3 | async-start | bytes 262144 | tf_op jit(solution)/shard_map/all_to_all | solution.py:90
Sparse Core Ops, SparseCore 0:
  8.9 48.1 all-gather.4
  58.7 22.3 all-gather.6
  82.7 34.4 all-gather.8
